TPU v7x, 32 devices: a whole 2x2x4 slice. The times are simulated.
32 devices in a mesh: own: 16 (over z, y, x), rep: 2 (over core).
Axes of the slice: x: 2, y: 2, z: 4, core: 2. Of those that a mesh axis runs over, the one named last changes fastest.
Arguments:
- sample_rows: bfloat16 [32768, 768], P(('own', 'rep'))
- destination: int32 [32768], P(('own', 'rep')), may hold values from 0 to 32767, as said below
- neighbours: int32 [32768, 4], P(('own', 'rep')), may hold values from 0 to 127, as said below
- centroids: bfloat16 [64, 2, 128, 768], P('own', 'rep'), may hold values from -6 to 6
Outputs:
- new_centroids: bfloat16 [64, 2, 128, 768], P('own', 'rep')
- row_cost: float32 [32768], P(('own', 'rep'))
Inputs may be any that keep to these rules, and one draw needn't show every extreme that they name: destination is a permutation. Numbering devices own-major (device t = own index * 2 + rep index), ingested row i of device s goes to device t = destination[i] // 1024, and the rows that device t receives from device s fill its positions s * 32 up to (s + 1) * 32 - 1; every device sends exactly 32 rows to every device. `neighbours`: each regrouped row on the device with own index o and rep index r lists 4 different blocks a * 2 + r with a inside the grid and o * 4 - 1 <= a <= o * 4 + 4.
All inputs are finite; a program needn't handle non-finite values.
Results may differ from a plain program's by a relative error of at most 0.0075.
Values may be sent and summed in bfloat16 or wider, within the bound.
A program may use at most 64 MiB of HBM per device.

v0:
```python
import math

import jax
import jax.numpy as jnp
from jax import lax
from jax.sharding import PartitionSpec as P

ITERS = 2


PRIOR = 1.0


def passed_along(array, axis, by):
    devices = lax.axis_size(axis)
    pairs = [(i, i + by) for i in range(devices) if 0 <= i + by < devices]
    return lax.ppermute(array, axis, pairs)


def padded_2(array, sides, width):
    for axis, dim in sides:
        devices, length = (lax.axis_size(axis), array.shape[dim])
        up = [(i, (i + 1) % devices) for i in range(devices - 1)]
        down = [(j, i) for i, j in up]
        last = lax.slice_in_dim(array, length - width, length, axis=dim)
        initial = lax.slice_in_dim(array, 0, width, axis=dim)
        before = lax.ppermute(last, axis, up)
        after = lax.ppermute(initial, axis, down)
        array = jnp.concatenate([before, array, after], axis=dim)
    return array


def soft_assign(local_rows, local_ids, candidates):
    window, per_block, features = candidates.shape
    flat_blocks = candidates.reshape(window * per_block, features)
    inv_scale = 0.5 / math.sqrt(features)
    cross = lax.dot_general(
        local_rows, flat_blocks, (((1,), (1,)), ((), ())), preferred_element_type=jnp.float32
    )
    cand_wide = flat_blocks.astype(jnp.float32)
    cand_norm = jnp.sum(cand_wide * cand_wide, axis=1)
    rows_wide = local_rows.astype(jnp.float32)
    rows_norm = jnp.sum(rows_wide * rows_wide, axis=1)
    logits = (2.0 * cross - rows_norm[:, None] - cand_norm[None, :]) * inv_scale
    logits = logits.reshape(local_rows.shape[0], window, per_block)
    slots = jnp.arange(window, dtype=jnp.int32)
    chosen = jnp.any(local_ids[:, :, None] == slots[None, None, :], axis=1)[:, :, None]
    masked = jnp.where(chosen, logits, -jnp.inf)
    row_top = jnp.max(masked, axis=(1, 2), keepdims=True)
    weights = jnp.where(chosen, jnp.exp(masked - row_top), 0.0)
    row_total = jnp.sum(weights, axis=(1, 2), keepdims=True)
    responses = weights / row_total
    row_cost = -(row_top[:, 0, 0] + jnp.log(row_total[:, 0, 0]))
    resp_half = responses.reshape(local_rows.shape[0], window * per_block).astype(jnp.bfloat16)
    part_sums = lax.dot_general(
        resp_half, local_rows, (((0,), (0,)), ((), ())), preferred_element_type=jnp.float32
    )
    part_counts = jnp.sum(responses, axis=0)
    return (part_sums.reshape(window, per_block, features), part_counts, row_cost)


def refresh(total, tally, previous):
    return ((total + PRIOR * previous.astype(jnp.float32)) / (tally[..., None] + PRIOR)).astype(
        jnp.bfloat16
    )


def settle_edges(part_sums, part_counts, current):
    blocks = part_sums.shape[0] - 2
    arrivals = []
    for shift_by, edge_index in ((1, blocks + 1), (-1, 0)):
        arrivals.append(
            (
                passed_along(part_sums[edge_index].astype(jnp.bfloat16), "own", shift_by).astype(
                    jnp.float32
                ),
                passed_along(part_counts[edge_index].astype(jnp.bfloat16), "own", shift_by).astype(
                    jnp.float32
                ),
            )
        )
    from_left, from_right = arrivals
    total = part_sums[1 : blocks + 1].at[0].add(from_left[0]).at[blocks - 1].add(from_right[0])
    tally = part_counts[1 : blocks + 1].at[0].add(from_left[1]).at[blocks - 1].add(from_right[1])
    return refresh(total, tally, current)


def per_device(sample_rows, destination, neighbours, centroids):
    own_count = lax.axis_size("own")
    rep_count = lax.axis_size("rep")
    count_rows, features = sample_rows.shape
    per_pair = count_rows // (own_count * rep_count)
    target = destination // count_rows
    slot_index = destination % per_pair
    outgoing = jnp.zeros((own_count, rep_count, per_pair, features), sample_rows.dtype)
    outgoing = outgoing.at[target // rep_count, target % rep_count, slot_index].set(sample_rows)
    arrived = lax.all_to_all(
        lax.all_to_all(outgoing, "own", split_axis=0, concat_axis=0, tiled=True),
        "rep",
        split_axis=1,
        concat_axis=1,
        tiled=True,
    )
    local_rows = arrived.reshape(count_rows, features)
    blocks = centroids.shape[0]
    per_block = centroids.shape[2]
    first_block = lax.axis_index("own") * blocks - 1
    local_ids = neighbours // rep_count - first_block
    current = centroids.reshape(blocks, per_block, features)
    padded = padded_2(centroids, (("own", 0),), 1)
    candidates = padded.reshape(blocks + 2, per_block, features)
    row_cost = jnp.zeros((count_rows,), jnp.float32)
    for iteration in range(ITERS):
        part_sums, part_counts, row_cost = soft_assign(local_rows, local_ids, candidates)
        if iteration + 1 == ITERS:
            current = settle_edges(part_sums, part_counts, current)
        else:
            current = settle_edges(part_sums, part_counts, current)
            padded = padded_2(current.reshape(blocks, 1, per_block, features), (("own", 0),), 1)
            candidates = padded.reshape(blocks + 2, per_block, features)
    return (current.reshape(centroids.shape), row_cost)


def solution(mesh):
    return jax.shard_map(
        per_device,
        mesh=mesh,
        in_specs=(
            P(("own", "rep"), None),
            P(("own", "rep")),
            P(("own", "rep"), None),
            P("own", "rep", None, None),
        ),
        out_specs=(P("own", "rep", None, None), P(("own", "rep"))),
        check_vma=False,
    )
```

profile of v0, /device:TPU:16, one launch (start us, length us, event | category | flops | bytes accessed | tf_op | source)
XLA Modules:
  0.0 139.1 jit_solution(12110478912115673623)
XLA Ops:
  0.6 0.7 compare_select_fusion.2
  1.3 0.7 and_reduce_fusion
  2.1 0.7 multiply_reduce_fusion.3
  2.8 7.0 %scatter_custom_fusion = bf16[1024,768]{1,0:T(8,128)(2,1)} fusion(s32[1024]{0:T(1024)S(1)} %broadcast_select_fusion, bf16[1024,768]{1,0:T(8,128)(2,1)} %param.20, bf16[]{:T(256)} %constant.261.clone.1), kind=kCustom, calls=%fused_computation.21 | custom fusion | bytes 1573376
  9.9 7.2 %all-to-all-start = ((bf16[16,2,32,768]{3,2,1,0:T(8,128)(2,1)}), bf16[16,2,32,768]{3,2,1,0:T(8,128)(2,1)S(1)}, u32[]{:S(2)}, u32[]{:S(2)}) async-start(bf16[16,2,32,768]{3,2,1,0:T(8,128)(2,1)} %bitcast.4), calls=%async_computation | async-start | bytes 3145728 | tf_op jit(solution)/shard_map/all_to_all | solution.py:98
  17.1 0.0 copy-done.2
  17.2 4.3 %collective-permute-start.1 = (bf16[1,1,128,768]{3,2,1,0:T(8,128)(2,1)S(1)}, bf16[1,1,128,768]{3,2,1,0:T(8,128)(2,1)S(1)}, u32[]{:S(2)}, u32[]{:S(2)}) collective-permute-start(bf16[1,1,128,768]{3,2,1,0:T(8,128)(2,1)S(1)} %get-tuple-element.124), channel_id=1, source_target_pairs={{2,0},{4,2},{6,4},{8,6},{10,8},{12,10},{14,12},{16,14},{18,16},{20... | collective-permute-start | bytes 589832 | tf_op jit(solution)/shard_map/ppermute | solution.py:28
  21.4 1.9 %collective-permute-start = (bf16[1,1,128,768]{3,2,1,0:T(8,128)(2,1)S(1)}, bf16[1,1,128,768]{3,2,1,0:T(8,128)(2,1)S(1)}, u32[]{:S(2)}, u32[]{:S(2)}) collective-permute-start(bf16[1,1,128,768]{3,2,1,0:T(8,128)(2,1)S(1)} %get-tuple-element.125), channel_id=1, source_target_pairs={{0,2},{2,4},{4,6},{6,8},{8,10},{10,12},{12,14},{14,16},{16,18},{18... | collective-permute-start | bytes 589832 | tf_op jit(solution)/shard_map/ppermute | solution.py:27
  23.4 0.0 copy-done.6
  23.4 0.1 fusion.19
  23.5 34.8 %collective-permute-done = bf16[1,1,128,768]{3,2,1,0:T(8,128)(2,1)S(1)} collective-permute-done((bf16[1,1,128,768]{3,2,1,0:T(8,128)(2,1)S(1)}, bf16[1,1,128,768]{3,2,1,0:T(8,128)(2,1)S(1)}, u32[]{:S(2)}, u32[]{:S(2)}) %collective-permute-start) | collective-permute-done | bytes 196640 | tf_op jit(solution)/shard_map/ppermute | solution.py:27
  58.3 0.1 constant_dynamic-update-slice_fusion.1
  58.4 0.0 collective-permute-done.1
  58.4 0.0 copy-start
  58.4 1.0 copy-done
  59.4 0.3 multiply_reduce_fusion.2
  59.7 0.0 all-to-all-done
  59.7 0.1 copy.50
  59.9 5.0 %all_to_all.10 = bf16[16,2,32,768]{3,2,0,1:T(8,128)(2,1)S(1)} all-to-all(bf16[16,2,32,768]{3,2,0,1:T(8,128)(2,1)S(1)} %copy.50), channel_id=1, replica_groups=mesh['own'=16,'rep'=2] {'rep'}, dimensions={1} | all-to-all | bytes 3145728 | tf_op jit(solution)/shard_map/all_to_all | solution.py:97
  64.9 0.4 multiply_reduce_fusion
  65.2 0.1 sub.89
  65.3 0.1 copy.51
  65.5 1.1 copy-done.1
  66.6 1.6 %fusion.29 = (f32[1024]{0:T(1024)S(1)}, f32[1024,768]{0,1:T(8,128)S(1)}) fusion(f32[768]{0:T(1024)S(1)} %bitcast.107, f32[1024]{0:T(1024)S(1)} %sub.89, pred[1024,6]{0,1:T(8,128)(4,1)S(1)} %fusion.19, bf16[1024,768]{1,0:T(8,128)(2,1)S(1)} %bitcast.98, bf16[768,768]{1,0:T(8,128)(2,1)S(1)} %bitcast.104), kind=kOutput, calls=%fused_computation.84 | convolution fusion | flops 1212677120 | bytes 5915648 | tf_op jit(solution)/shard_map/dot_general | solution.py:37
  68.2 1.1 fusion.1
  69.3 1.4 %fusion.32 = (f32[768]{0:T(1024)S(1)}, bf16[1024,768]{0,1:T(8,128)(2,1)S(1)}) fusion(f32[1024]{0:T(1024)S(1)} %fusion.1, f32[1024]{0:T(1024)S(1)} %get-tuple-element.133, f32[768]{0:T(1024)S(1)} %bitcast.109, f32[1024]{0:T(1024)S(1)} %sub.89, f32[1024,768]{0,1:T(8,128)S(1)} %get-tuple-element.134, pred[1024,6]{0,1:T(8,128)(4,1)S(1)} %fusion.19), kind=kLoop, calls=%fused_computation.86 | loop fusion | flops 7863552 | bytes 4743168 | tf_op jit(solution)/shard_map/reduce_sum | solution.py:58
  70.7 2.8 %collective-permute-start.5 = (bf16[128]{0:T(256)(128)(2,1)S(1)}, bf16[128]{0:T(256)(128)(2,1)S(1)}, u32[]{:S(2)}, u32[]{:S(2)}) collective-permute-start(bf16[128]{0:T(256)(128)(2,1)S(1)} %get-tuple-element.131), channel_id=1, source_target_pairs={{2,0},{4,2},{6,4},{8,6},{10,8},{12,10},{14,12},{16,14},{18,16},{20... | collective-permute-start | bytes 776 | tf_op jit(solution)/shard_map/ppermute | solution.py:17
  73.5 3.1 %collective-permute-start.4 = (bf16[128]{0:T(256)(128)(2,1)S(1)}, bf16[128]{0:T(256)(128)(2,1)S(1)}, u32[]{:S(2)}, u32[]{:S(2)}) collective-permute-start(bf16[128]{0:T(256)(128)(2,1)S(1)} %get-tuple-element.132), channel_id=1, source_target_pairs={{0,2},{2,4},{4,6},{6,8},{8,10},{10,12},{12,14},{14,16},{16,18},{18... | collective-permute-start | bytes 776 | tf_op jit(solution)/shard_map/ppermute | solution.py:17
  76.6 1.4 %fusion.39 = (bf16[768,768]{1,0:T(8,128)(2,1)S(1)}, f32[768,768]{1,0:T(8,128)S(1)}) fusion(bf16[1024,768]{1,0:T(8,128)(2,1)S(1)} %bitcast.99, bf16[1024,768]{0,1:T(8,128)(2,1)S(1)} %get-tuple-element.117), kind=kOutput, calls=%fused_computation.92 | convolution fusion | flops 1208549376 | bytes 6684672 | tf_op jit(solution)/shard_map/dot_general | solution.py:55
  78.0 4.6 %collective-permute-start.3 = (bf16[128,768]{1,0:T(8,128)(2,1)S(1)}, bf16[128,768]{1,0:T(8,128)(2,1)S(1)}, u32[]{:S(2)}, u32[]{:S(2)}) collective-permute-start(bf16[128,768]{1,0:T(8,128)(2,1)S(1)} %get-tuple-element.120), channel_id=1, source_target_pairs={{2,0},{4,2},{6,4},{8,6},{10,8},{12,10},{14,12},{16,14},{18,16},{20... | collective-permute-start | bytes 589832 | tf_op jit(solution)/shard_map/ppermute | solution.py:17
  82.6 1.9 %collective-permute-start.2 = (bf16[128,768]{1,0:T(8,128)(2,1)S(1)}, bf16[128,768]{1,0:T(8,128)(2,1)S(1)}, u32[]{:S(2)}, u32[]{:S(2)}) collective-permute-start(bf16[128,768]{1,0:T(8,128)(2,1)S(1)} %get-tuple-element.121), channel_id=1, source_target_pairs={{0,2},{2,4},{4,6},{6,8},{8,10},{10,12},{12,14},{14,16},{16,18},{18... | collective-permute-start | bytes 589832 | tf_op jit(solution)/shard_map/ppermute | solution.py:17
  84.5 1.3 slice.288
  85.8 0.0 copy-done.5
  85.8 0.0 collective-permute-done.4
  85.8 0.0 collective-permute-done.5
  85.9 6.5 %collective-permute-done.2 = bf16[128,768]{1,0:T(8,128)(2,1)S(1)} collective-permute-done((bf16[128,768]{1,0:T(8,128)(2,1)S(1)}, bf16[128,768]{1,0:T(8,128)(2,1)S(1)}, u32[]{:S(2)}, u32[]{:S(2)}) %collective-permute-start.2) | collective-permute-done | bytes 196640 | tf_op jit(solution)/shard_map/ppermute | solution.py:17
  92.4 1.8 %fusion.18 = f32[4,128,768]{2,1,0:T(8,128)} fusion(f32[4,128,768]{2,1,0:T(8,128)} %bitcast.8, f32[768,768]{1,0:T(8,128)} %copy-done.5, bf16[128,768]{1,0:T(8,128)(2,1)S(1)} %collective-permute-done.2), kind=kLoop, calls=%fused_computation.33 | loop fusion | flops 196608 | bytes 983040 | tf_op jit(solution)/shard_map/scatter-add | solution.py:83
  94.2 0.0 collective-permute-done.3
  94.2 1.8 %fusion.16 = f32[4,128,768]{2,1,0:T(8,128)} fusion(f32[4,128,768]{2,1,0:T(8,128)} %fusion.18, bf16[128,768]{1,0:T(8,128)(2,1)S(1)} %collective-permute-done.3), kind=kLoop, calls=%fused_computation.30 | loop fusion | flops 196608 | bytes 983040 | tf_op jit(solution)/shard_map/scatter-add | solution.py:83
  95.9 0.0 copy-done.3
  95.9 1.6 %fusion.5 = bf16[4,128,768]{2,1,0:T(8,128)(2,1)S(1)} fusion(f32[4,128,768]{2,1,0:T(8,128)} %fusion.16, bf16[4,1,128,768]{3,2,1,0:T(8,128)(2,1)S(1)} %copy-done.3, f32[4,128]{1,0:T(4,128)S(1)} %add_bitcast_fusion.1), kind=kLoop, calls=%fused_computation.14 | loop fusion | flops 1572864 | bytes 3147776 | tf_op jit(solution)/shard_map/convert_element_type | solution.py:63
  97.6 1.9 %collective-permute-start.6 = (bf16[1,1,128,768]{3,2,0,1:T(8,128)(2,1)S(1)}, bf16[1,1,128,768]{3,2,0,1:T(8,128)(2,1)S(1)}, u32[]{:S(2)}, u32[]{:S(2)}) collective-permute-start(bf16[1,1,128,768]{3,2,0,1:T(8,128)(2,1)S(1)} %get-tuple-element.122), channel_id=1, source_target_pairs={{0,2},{2,4},{4,6},{6,8},{8,10},{10,12},{12,14},{14,16},{16,18},{18... | collective-permute-start | bytes 589832 | tf_op jit(solution)/shard_map/ppermute | solution.py:27
  99.5 5.9 %collective-permute-start.7 = (bf16[1,1,128,768]{3,2,1,0:T(8,128)(2,1)S(1)}, bf16[1,1,128,768]{3,2,1,0:T(8,128)(2,1)S(1)}, u32[]{:S(2)}, u32[]{:S(2)}) collective-permute-start(bf16[1,1,128,768]{3,2,1,0:T(8,128)(2,1)S(1)} %get-tuple-element.123), channel_id=1, source_target_pairs={{2,0},{4,2},{6,4},{8,6},{10,8},{12,10},{14,12},{16,14},{18,16},{20... | collective-permute-start | bytes 589832 | tf_op jit(solution)/shard_map/ppermute | solution.py:28
  105.4 1.6 %collective-permute-done.6 = bf16[1,1,128,768]{3,2,0,1:T(8,128)(2,1)S(1)} collective-permute-done((bf16[1,1,128,768]{3,2,0,1:T(8,128)(2,1)S(1)}, bf16[1,1,128,768]{3,2,0,1:T(8,128)(2,1)S(1)}, u32[]{:S(2)}, u32[]{:S(2)}) %collective-permute-start.6) | collective-permute-done | bytes 196640 | tf_op jit(solution)/shard_map/ppermute | solution.py:27
  107.0 1.4 %collective-permute-done.7 = bf16[1,1,128,768]{3,2,1,0:T(8,128)(2,1)S(1)} collective-permute-done((bf16[1,1,128,768]{3,2,1,0:T(8,128)(2,1)S(1)}, bf16[1,1,128,768]{3,2,1,0:T(8,128)(2,1)S(1)}, u32[]{:S(2)}, u32[]{:S(2)}) %collective-permute-start.7) | collective-permute-done | bytes 196640 | tf_op jit(solution)/shard_map/ppermute | solution.py:28
  108.4 0.3 multiply_reduce_fusion.1
  108.7 1.6 %fusion.40 = (f32[1024]{0:T(1024)S(1)}, f32[1024,768]{0,1:T(8,128)S(1)}) fusion(f32[768]{0:T(1024)S(1)} %bitcast.116, f32[1024]{0:T(1024)S(1)} %sub.89, bf16[1024,768]{1,0:T(8,128)(2,1)S(1)} %bitcast.100, bf16[768,768]{1,0:T(8,128)(2,1)S(1)} %bitcast.105, pred[1024,6]{0,1:T(8,128)(4,1)S(1)} %fusion.19), kind=kOutput, calls=%fused_computation.93 | convolution fusion | flops 1212677120 | bytes 5915648 | tf_op jit(solution)/shard_map/dot_general | solution.py:37
  110.3 0.6 fusion.3
  110.9 0.8 fusion.30
  111.6 0.6 add_negate_fusion
  112.3 6.2 %collective-permute-start.11 = (bf16[128]{0:T(256)(128)(2,1)S(1)}, bf16[128]{0:T(256)(128)(2,1)S(1)}, u32[]{:S(2)}, u32[]{:S(2)}) collective-permute-start(bf16[128]{0:T(256)(128)(2,1)S(1)} %get-tuple-element.129), channel_id=1, source_target_pairs={{2,0},{4,2},{6,4},{8,6},{10,8},{12,10},{14,12},{16,14},{18,16},{20... | collective-permute-start | bytes 776 | tf_op jit(solution)/shard_map/ppermute | solution.py:17
  118.5 1.9 %collective-permute-start.10 = (bf16[128]{0:T(256)(128)(2,1)S(1)}, bf16[128]{0:T(256)(128)(2,1)S(1)}, u32[]{:S(2)}, u32[]{:S(2)}) collective-permute-start(bf16[128]{0:T(256)(128)(2,1)S(1)} %get-tuple-element.130), channel_id=1, source_target_pairs={{0,2},{2,4},{4,6},{6,8},{8,10},{10,12},{12,14},{14,16},{16,18},{18... | collective-permute-start | bytes 776 | tf_op jit(solution)/shard_map/ppermute | solution.py:17
  120.4 1.4 %fusion.41 = (bf16[768,768]{1,0:T(8,128)(2,1)S(1)}, f32[768,768]{1,0:T(8,128)S(1)}) fusion(bf16[1024,768]{1,0:T(8,128)(2,1)S(1)} %bitcast.101, bf16[1024,768]{0,1:T(8,128)(2,1)S(1)} %get-tuple-element.113), kind=kOutput, calls=%fused_computation.94 | convolution fusion | flops 1208549376 | bytes 6684672 | tf_op jit(solution)/shard_map/dot_general | solution.py:55
  121.8 5.7 %collective-permute-start.9 = (bf16[128,768]{1,0:T(8,128)(2,1)S(1)}, bf16[128,768]{1,0:T(8,128)(2,1)S(1)}, u32[]{:S(2)}, u32[]{:S(2)}) collective-permute-start(bf16[128,768]{1,0:T(8,128)(2,1)S(1)} %get-tuple-element.118), channel_id=1, source_target_pairs={{2,0},{4,2},{6,4},{8,6},{10,8},{12,10},{14,12},{16,14},{18,16},{20... | collective-permute-start | bytes 589832 | tf_op jit(solution)/shard_map/ppermute | solution.py:17
  127.6 1.9 %collective-permute-start.8 = (bf16[128,768]{1,0:T(8,128)(2,1)S(1)}, bf16[128,768]{1,0:T(8,128)(2,1)S(1)}, u32[]{:S(2)}, u32[]{:S(2)}) collective-permute-start(bf16[128,768]{1,0:T(8,128)(2,1)S(1)} %get-tuple-element.119), channel_id=1, source_target_pairs={{0,2},{2,4},{4,6},{6,8},{8,10},{10,12},{12,14},{14,16},{16,18},{18... | collective-permute-start | bytes 589832 | tf_op jit(solution)/shard_map/ppermute | solution.py:17
  129.5 0.1 slice.295
  129.6 0.0 copy-done.4
  129.6 0.0 collective-permute-done.10
  129.7 0.0 collective-permute-done.11
  129.7 7.2 %collective-permute-done.8 = bf16[128,768]{1,0:T(8,128)(2,1)S(1)} collective-permute-done((bf16[128,768]{1,0:T(8,128)(2,1)S(1)}, bf16[128,768]{1,0:T(8,128)(2,1)S(1)}, u32[]{:S(2)}, u32[]{:S(2)}) %collective-permute-start.8) | collective-permute-done | bytes 196640 | tf_op jit(solution)/shard_map/ppermute | solution.py:17
  136.9 1.0 fusion.15
  138.0 0.0 collective-permute-done.9
  138.0 0.1 fusion.13
  138.0 1.1 fusion.12
  (31 shorter events, 0.4 us)
Async XLA Ops:
  9.9 7.3 %copy-start.2 = (bf16[4,1,128,768]{3,2,1,0:T(8,128)(2,1)S(1)}, bf16[4,1,128,768]{3,2,1,0:T(8,128)(2,1)}, u32[]{:S(2)}) copy-start(bf16[4,1,128,768]{3,2,1,0:T(8,128)(2,1)} %param.23) | copy-start | bytes 2359300
  9.9 13.5 %copy-start.6 = (s32[1024,4]{0,1:T(4,128)S(1)}, s32[1024,4]{0,1:T(4,128)}, u32[]{:S(2)}) copy-start(s32[1024,4]{0,1:T(4,128)} %param.22) | copy-start | bytes 49156
  9.9 49.9 %all-to-all-start = ((bf16[16,2,32,768]{3,2,1,0:T(8,128)(2,1)}), bf16[16,2,32,768]{3,2,1,0:T(8,128)(2,1)S(1)}, u32[]{:S(2)}, u32[]{:S(2)}) async-start(bf16[16,2,32,768]{3,2,1,0:T(8,128)(2,1)} %bitcast.4), calls=%async_computation | async-start | bytes 3145728 | tf_op jit(solution)/shard_map/all_to_all | solution.py:98
  17.2 41.2 %collective-permute-start.1 = (bf16[1,1,128,768]{3,2,1,0:T(8,128)(2,1)S(1)}, bf16[1,1,128,768]{3,2,1,0:T(8,128)(2,1)S(1)}, u32[]{:S(2)}, u32[]{:S(2)}) collective-permute-start(bf16[1,1,128,768]{3,2,1,0:T(8,128)(2,1)S(1)} %get-tuple-element.124), channel_id=1, source_target_pairs={{2,0},{4,2},{6,4},{8,6},{10,8},{12,10},{14,12},{16,14},{18,16},{20... | collective-permute-start | bytes 589832 | tf_op jit(solution)/shard_map/ppermute | solution.py:28
  21.4 36.9 %collective-permute-start = (bf16[1,1,128,768]{3,2,1,0:T(8,128)(2,1)S(1)}, bf16[1,1,128,768]{3,2,1,0:T(8,128)(2,1)S(1)}, u32[]{:S(2)}, u32[]{:S(2)}) collective-permute-start(bf16[1,1,128,768]{3,2,1,0:T(8,128)(2,1)S(1)} %get-tuple-element.125), channel_id=1, source_target_pairs={{0,2},{2,4},{4,6},{6,8},{8,10},{10,12},{12,14},{14,16},{16,18},{18... | collective-permute-start | bytes 589832 | tf_op jit(solution)/shard_map/ppermute | solution.py:27
  58.4 1.0 copy-start
  65.3 1.3 copy-start.1
  70.7 15.1 %collective-permute-start.5 = (bf16[128]{0:T(256)(128)(2,1)S(1)}, bf16[128]{0:T(256)(128)(2,1)S(1)}, u32[]{:S(2)}, u32[]{:S(2)}) collective-permute-start(bf16[128]{0:T(256)(128)(2,1)S(1)} %get-tuple-element.131), channel_id=1, source_target_pairs={{2,0},{4,2},{6,4},{8,6},{10,8},{12,10},{14,12},{16,14},{18,16},{20... | collective-permute-start | bytes 776 | tf_op jit(solution)/shard_map/ppermute | solution.py:17
  73.5 12.3 %collective-permute-start.4 = (bf16[128]{0:T(256)(128)(2,1)S(1)}, bf16[128]{0:T(256)(128)(2,1)S(1)}, u32[]{:S(2)}, u32[]{:S(2)}) collective-permute-start(bf16[128]{0:T(256)(128)(2,1)S(1)} %get-tuple-element.132), channel_id=1, source_target_pairs={{0,2},{2,4},{4,6},{6,8},{8,10},{10,12},{12,14},{14,16},{16,18},{18... | collective-permute-start | bytes 776 | tf_op jit(solution)/shard_map/ppermute | solution.py:17
  78.0 7.8 %copy-start.5 = (f32[768,768]{1,0:T(8,128)}, f32[768,768]{1,0:T(8,128)S(1)}, u32[]{:S(2)}) copy-start(f32[768,768]{1,0:T(8,128)S(1)} %get-tuple-element.136) | copy-start | bytes 7077892
  78.0 16.1 %collective-permute-start.3 = (bf16[128,768]{1,0:T(8,128)(2,1)S(1)}, bf16[128,768]{1,0:T(8,128)(2,1)S(1)}, u32[]{:S(2)}, u32[]{:S(2)}) collective-permute-start(bf16[128,768]{1,0:T(8,128)(2,1)S(1)} %get-tuple-element.120), channel_id=1, source_target_pairs={{2,0},{4,2},{6,4},{8,6},{10,8},{12,10},{14,12},{16,14},{18,16},{20... | collective-permute-start | bytes 589832 | tf_op jit(solution)/shard_map/ppermute | solution.py:17
  82.6 9.8 %collective-permute-start.2 = (bf16[128,768]{1,0:T(8,128)(2,1)S(1)}, bf16[128,768]{1,0:T(8,128)(2,1)S(1)}, u32[]{:S(2)}, u32[]{:S(2)}) collective-permute-start(bf16[128,768]{1,0:T(8,128)(2,1)S(1)} %get-tuple-element.121), channel_id=1, source_target_pairs={{0,2},{2,4},{4,6},{6,8},{8,10},{10,12},{12,14},{14,16},{16,18},{18... | collective-permute-start | bytes 589832 | tf_op jit(solution)/shard_map/ppermute | solution.py:17
  85.8 10.1 %copy-start.3 = (bf16[4,1,128,768]{3,2,1,0:T(8,128)(2,1)S(1)}, bf16[4,1,128,768]{3,2,1,0:T(8,128)(2,1)}, u32[]{:S(2)}) copy-start(bf16[4,1,128,768]{3,2,1,0:T(8,128)(2,1)} %param.23) | copy-start | bytes 2359300
  97.6 9.4 %collective-permute-start.6 = (bf16[1,1,128,768]{3,2,0,1:T(8,128)(2,1)S(1)}, bf16[1,1,128,768]{3,2,0,1:T(8,128)(2,1)S(1)}, u32[]{:S(2)}, u32[]{:S(2)}) collective-permute-start(bf16[1,1,128,768]{3,2,0,1:T(8,128)(2,1)S(1)} %get-tuple-element.122), channel_id=1, source_target_pairs={{0,2},{2,4},{4,6},{6,8},{8,10},{10,12},{12,14},{14,16},{16,18},{18... | collective-permute-start | bytes 589832 | tf_op jit(solution)/shard_map/ppermute | solution.py:27
  99.5 8.9 %collective-permute-start.7 = (bf16[1,1,128,768]{3,2,1,0:T(8,128)(2,1)S(1)}, bf16[1,1,128,768]{3,2,1,0:T(8,128)(2,1)S(1)}, u32[]{:S(2)}, u32[]{:S(2)}) collective-permute-start(bf16[1,1,128,768]{3,2,1,0:T(8,128)(2,1)S(1)} %get-tuple-element.123), channel_id=1, source_target_pairs={{2,0},{4,2},{6,4},{8,6},{10,8},{12,10},{14,12},{16,14},{18,16},{20... | collective-permute-start | bytes 589832 | tf_op jit(solution)/shard_map/ppermute | solution.py:28
  112.3 17.4 %collective-permute-start.11 = (bf16[128]{0:T(256)(128)(2,1)S(1)}, bf16[128]{0:T(256)(128)(2,1)S(1)}, u32[]{:S(2)}, u32[]{:S(2)}) collective-permute-start(bf16[128]{0:T(256)(128)(2,1)S(1)} %get-tuple-element.129), channel_id=1, source_target_pairs={{2,0},{4,2},{6,4},{8,6},{10,8},{12,10},{14,12},{16,14},{18,16},{20... | collective-permute-start | bytes 776 | tf_op jit(solution)/shard_map/ppermute | solution.py:17
  118.5 11.2 %collective-permute-start.10 = (bf16[128]{0:T(256)(128)(2,1)S(1)}, bf16[128]{0:T(256)(128)(2,1)S(1)}, u32[]{:S(2)}, u32[]{:S(2)}) collective-permute-start(bf16[128]{0:T(256)(128)(2,1)S(1)} %get-tuple-element.130), channel_id=1, source_target_pairs={{0,2},{2,4},{4,6},{6,8},{8,10},{10,12},{12,14},{14,16},{16,18},{18... | collective-permute-start | bytes 776 | tf_op jit(solution)/shard_map/ppermute | solution.py:17
  121.8 7.8 %copy-start.4 = (f32[768,768]{1,0:T(8,128)}, f32[768,768]{1,0:T(8,128)S(1)}, u32[]{:S(2)}) copy-start(f32[768,768]{1,0:T(8,128)S(1)} %get-tuple-element.140) | copy-start | bytes 7077892
  121.8 16.1 %collective-permute-start.9 = (bf16[128,768]{1,0:T(8,128)(2,1)S(1)}, bf16[128,768]{1,0:T(8,128)(2,1)S(1)}, u32[]{:S(2)}, u32[]{:S(2)}) collective-permute-start(bf16[128,768]{1,0:T(8,128)(2,1)S(1)} %get-tuple-element.118), channel_id=1, source_target_pairs={{2,0},{4,2},{6,4},{8,6},{10,8},{12,10},{14,12},{16,14},{18,16},{20... | collective-permute-start | bytes 589832 | tf_op jit(solution)/shard_map/ppermute | solution.py:17
  127.6 9.4 %collective-permute-start.8 = (bf16[128,768]{1,0:T(8,128)(2,1)S(1)}, bf16[128,768]{1,0:T(8,128)(2,1)S(1)}, u32[]{:S(2)}, u32[]{:S(2)}) collective-permute-start(bf16[128,768]{1,0:T(8,128)(2,1)S(1)} %get-tuple-element.119), channel_id=1, source_target_pairs={{0,2},{2,4},{4,6},{6,8},{8,10},{10,12},{12,14},{14,16},{16,18},{18... | collective-permute-start | bytes 589832 | tf_op jit(solution)/shard_map/ppermute | solution.py:17
where the time goes:
time: 140 us; the launch traced here: 139 us
  waiting for transfers between devices  51.5 us (37%)
  starting transfers between devices  49.3 us (35%)
  other arithmetic  15.1 us (11%)
  local copies, waits for them, and re-layouts  11.3 us (8%)
  matrix products  5.92 us (4%)
  blocking collectives  5 us (4%)
    ppermute x2, waiting for transfers between devices, padded_2(): before = lax.ppermute(last, axis, up)  36.4 us
    ppermute x8, starting transfers between devices, passed_along(): return lax.ppermute(array, axis, pairs)  28.1 us
    ppermute x8, waiting for transfers between devices, passed_along(): return lax.ppermute(array, axis, pairs)  13.7 us
    ppermute x2, starting transfers between devices, padded_2(): after = lax.ppermute(initial, axis, down)  10.2 us
    unnamed x17, local copies, waits for them, and re-layouts  9.27 us
    all_to_all x1, starting transfers between devices, per_device(): lax.all_to_all(outgoing, 'own', split_axis=0, concat_axis=0, tiled=True)  7.24 us
    all_to_all x1, blocking collectives, per_device(): lax.all_to_all(lax.all_to_all(outgoing, 'own', split_axis=0, concat_axis=...  5 us
    scatter-add x4, other arithmetic, settle_edges(): part_sums[1:blocks + 1].at[0].add(from_left[0]).at[blocks - 1]  4.64 us
  transfers between devices with their start and end apart: 13, of which 5 were waited for; matrix products, arithmetic and copies ran while one was open for 6% of the time, Pallas kernels for 0%

commit v1 on v0

v1 whole, which is shorter than its diff:
```python
import functools
import math

import jax
import jax.numpy as jnp
from jax import lax
from jax.experimental import pallas as pl
from jax.experimental.pallas import tpu as pltpu
from jax.sharding import PartitionSpec as P

ITERS = 2
PRIOR = 1.0
MESH = pl.DeviceIdType.MESH
F32 = jnp.float32
BF16 = jnp.bfloat16
LN2 = math.log(2.0)
NT = (((1,), (1,)), ((), ()))
NN = (((1,), (0,)), ((), ()))


def dot(a, b, dims):
    return lax.dot_general(a, b, dims, preferred_element_type=F32)


def kernel(
    fused, own_n, rep_n, pp, chunk, order, *refs
):
    (nbr_ref, dest_ref, rows_ref, cent_ref, out_ref, cost_ref,
     arr, outb, cand, cn, bias, xn, acc, macc, lg, resp, snd, rcv, msnd, mrcv,
     a_send, a_recv, c_send, c_recv, s_send, s_recv, m_send, m_recv) = refs
    count, feat = rows_ref.shape
    slots = nbr_ref.shape[0]
    cb = rcv.shape[2]
    blk = cent_ref.shape[0] // cb
    win = blk + 2
    wc = win * cb
    nchunk = count // chunk
    total_n = own_n * rep_n
    own = lax.axis_index("own")
    rep = lax.axis_index("rep")
    me = own * rep_n + rep
    sides = (own > 0, own < own_n - 1)
    scale2 = 0.5 / math.sqrt(feat) / LN2

    barrier = pltpu.get_barrier_semaphore()
    if fused:
        def greet(k, carry):
            t = lax.rem(me + k, total_n)
            pl.semaphore_signal(
                barrier, inc=1, device_id=(lax.div(t, rep_n), lax.rem(t, rep_n)), device_id_type=MESH
            )
            return carry

        lax.fori_loop(1, total_n, greet, 0)
    else:
        for d in range(2):
            @pl.when(sides[d])
            def _():
                pl.semaphore_signal(
                    barrier, inc=1, device_id=(own + 2 * d - 1, rep), device_id_type=MESH
                )

    zero_block = jnp.zeros((cb, feat), BF16)
    for d in range(2):
        @pl.when(jnp.logical_not(sides[1 - d]))
        def _():
            place = 0 if d else win - 1
            cand[place * cb : (place + 1) * cb, :] = zero_block
            for q in range(3):
                rcv[d, q] = zero_block
                mrcv[d, q] = jnp.zeros((8, 128), F32)
    cand[cb : (blk + 1) * cb, :] = cent_ref[...]

    def block_copy(d):
        src = 0 if d == 0 else (blk - 1) * cb
        dst = (win - 1) * cb if d == 0 else 0
        return pltpu.make_async_remote_copy(
            src_ref=cent_ref.at[pl.ds(src, cb)],
            dst_ref=cand.at[pl.ds(dst, cb)],
            send_sem=c_send.at[d],
            recv_sem=c_recv.at[d],
            device_id=(own + 2 * d - 1, rep),
            device_id_type=MESH,
        )

    def edge_copies(d, q):
        where = (own + 2 * d - 1, rep)
        return [
            pltpu.make_async_remote_copy(
                src_ref=a.at[d, q], dst_ref=b.at[d, q], send_sem=s.at[d, q], recv_sem=r.at[d, q],
                device_id=where, device_id_type=MESH,
            )
            for a, b, s, r in ((msnd, mrcv, m_send, m_recv), (snd, rcv, s_send, s_recv))
        ]

    def row_copy(src, t):
        return pltpu.make_async_remote_copy(
            src_ref=outb.at[pl.ds(pl.multiple_of(t * pp, pp), pp)],
            dst_ref=arr.at[pl.ds(pl.multiple_of(src * pp, pp), pp)],
            send_sem=a_send.at[t],
            recv_sem=a_recv.at[src],
            device_id=(lax.div(t, rep_n), lax.rem(t, rep_n)),
            device_id_type=MESH,
        )

    per = chunk // pp if fused else 1
    group = lax.div(me, per) if fused else 0

    def pack(g):
        base = pl.multiple_of(g * chunk, chunk)
        pos = lax.broadcasted_iota(jnp.int32, (chunk, count), 0)
        bits = pp.bit_length() - 1
        want = lax.shift_right_logical(pos, bits) * count + (pos & (pp - 1))
        hot = dest_ref[...] - (g * per * count + me * pp)
        pick = jnp.where(want == hot, 1.0, 0.0).astype(BF16)
        outb[pl.ds(base, chunk), :] = dot(pick, rows_ref[...], NN).astype(BF16)

    def wait_entry():
        if fused:
            pl.semaphore_wait(barrier, total_n - 1)
        else:
            for d in range(2):
                @pl.when(sides[d])
                def _():
                    pl.semaphore_wait(barrier, 1)
        for d in range(2):
            @pl.when(sides[d])
            def _():
                block_copy(d).start()

    def send_group(g):
        def send(k, carry):
            t = g * per + lax.rem(me + k, per)

            @pl.when(t != me)
            def _():
                row_copy(me, t).start()

            return carry

        lax.fori_loop(0, per, send, 0)

    if fused:
        for n, j in enumerate(order):
            g = lax.rem(group + j, nchunk)
            pack(g)
            if n == 0:
                wait_entry()
            send_group(g)
        mine = pl.ds(pl.multiple_of(me * pp, pp), pp)
        arr[mine, :] = outb[mine, :]
        rows = arr
    else:
        wait_entry()
        rows = rows_ref

    for c in range(nchunk):
        ids = nbr_ref[:, c * chunk : (c + 1) * chunk]
        for w in range(win):
            block = (own * blk - 1 + w) * rep_n + rep
            hit = ids[0:1] == block
            for m in range(1, slots):
                hit = jnp.logical_or(hit, ids[m : m + 1] == block)
            bias[c, w : w + 1, :] = jnp.where(hit, 0.0, -jnp.inf)

    acc[...] = jnp.zeros_like(acc)
    macc[...] = jnp.zeros_like(macc)

    def norms(low, high):
        wide = cand[low:high, :].astype(F32)
        cn[low:high, :] = jnp.sum(wide * wide, axis=1, keepdims=True) * scale2

    norms(cb, (blk + 1) * cb)
    for d in range(2):
        @pl.when(sides[1 - d])
        def _():
            block_copy(d).wait_recv()
    norms(0, cb)
    norms(wc - cb, wc)

    def respond(c):
        raw = [lg[c, w * cb : (w + 1) * cb, :] + bias[c, w : w + 1, :] for w in range(win)]
        top = functools.reduce(jnp.maximum, raw)
        top = jnp.max(top, axis=0, keepdims=True)
        raw = [jnp.exp2(r - top) for r in raw]
        whole = jnp.sum(functools.reduce(jnp.add, raw), axis=0, keepdims=True)
        inverse = 1.0 / whole
        for w in range(win):
            part = slice(w * cb, (w + 1) * cb)
            got = raw[w] * inverse
            resp[c, part, :] = got.astype(BF16)
            folded = got[:, 0:128]
            for i in range(1, chunk // 128):
                folded = folded + got[:, i * 128 : (i + 1) * 128]
            macc[part, :] += folded
        return top, whole

    def chunk_rows(c):
        return rows[pl.ds(pl.multiple_of(c * chunk, chunk), chunk), :]

    def arrive(c):
        if fused:
            def wait(k, carry):
                s = c * per + k

                @pl.when(s != me)
                def _():
                    row_copy(s, s).wait_recv()

                return carry

            lax.fori_loop(0, per, wait, 0)
        x = chunk_rows(c)
        lg[c] = dot(cand[...], x, NT) * (2.0 * scale2) - cn[...]
        respond(c)
        wide = x.astype(F32)
        wide = wide * wide
        high = wide.astype(BF16)
        low = (wide - high.astype(F32)).astype(BF16)
        ones = jnp.ones((8, feat), BF16)
        xn[c] = dot(ones, high, NT) + dot(ones, low, NT)

    def early(j, carry):
        c = lax.rem(group + j, nchunk)
        arrive(c)
        acc[...] += dot(resp[c], chunk_rows(c), NN)
        return carry

    if nchunk > 1:
        lax.fori_loop(0, nchunk - 1, early, 0)
    last = lax.rem(group + nchunk - 1, nchunk)
    arrive(last)

    def part_of(w):
        return slice(w * cb, (w + 1) * cb)

    def mass_of(w):
        return jnp.sum(macc[part_of(w), :], axis=1, keepdims=True)

    def ship(d, q, w):
        snd[d, q] = acc[part_of(w), :].astype(BF16)
        wide = jnp.transpose(jnp.broadcast_to(mass_of(w), (cb, 128)))
        msnd[d, q] = wide[0:8, :]

        @pl.when(sides[d])
        def _():
            for copy in edge_copies(d, q):
                copy.start()

    def land(d, q):
        @pl.when(sides[1 - d])
        def _():
            for copy in edge_copies(d, q):
                copy.wait_recv()

    def fresh(w, source=None):
        total = acc[part_of(w), :] + cand[part_of(w), :].astype(F32)
        tally = mass_of(w) + PRIOR
        if source is not None:
            total = total + rcv[source].astype(F32)
            arrived = jnp.transpose(jnp.broadcast_to(mrcv[source][0:1, :], (128, 128)))
            tally = tally + arrived[:, 0:1]
        return (total * (1.0 / tally)).astype(BF16)

    def finish(w):
        acc[part_of(w), :] += dot(resp[last, part_of(w), :], chunk_rows(last), NN)

    def score(w):
        norms(w * cb, (w + 1) * cb)
        for c in range(nchunk):
            lg[c, part_of(w), :] = (
                dot(cand[part_of(w), :], chunk_rows(c), NT) * (2.0 * scale2) - cn[part_of(w), :]
            )

    for d, q, w in ((0, 0, 0), (1, 0, win - 1), (0, 1, 1), (1, 1, win - 2)):
        finish(w)
        ship(d, q, w)
    for w in range(2, win - 2):
        finish(w)
    for w in range(2, win - 2):
        cand[part_of(w), :] = fresh(w)
        score(w)
    for d, q, w in ((1, 0, 1), (0, 0, win - 2), (1, 1, 0), (0, 1, win - 1)):
        land(d, q)
        cand[part_of(w), :] = fresh(w, (d, q))
        score(w)

    macc[...] = jnp.zeros_like(macc)

    def second(c, carry):
        top, whole = respond(c)
        cost_ref[pl.ds(c, 1), :] = xn[c][0:1, :] * (scale2 * LN2) - (top * LN2 + jnp.log(whole))
        return carry

    lax.fori_loop(0, nchunk, second, 0)

    def gather(w):
        sums = dot(resp[0, part_of(w), :], chunk_rows(0), NN)
        for c in range(1, nchunk):
            sums = sums + dot(resp[c, part_of(w), :], chunk_rows(c), NN)
        acc[part_of(w), :] = sums

    for d, w in ((0, 0), (1, win - 1)):
        gather(w)
        ship(d, 2, w)
    for w in range(1, win - 1):
        gather(w)
    for w in range(2, win - 2):
        out_ref[part_of(w - 1), :] = fresh(w)
    for d, w in ((1, 1), (0, win - 2)):
        land(d, 2)
        out_ref[part_of(w - 1), :] = fresh(w, (d, 2))

    for d in range(2):
        @pl.when(sides[d])
        def _():
            block_copy(d).wait_send()
            for q in range(3):
                for copy in edge_copies(d, q):
                    copy.wait_send()

    if fused:
        def drain(k, carry):
            row_copy(me, lax.rem(me + k, total_n)).wait_send()
            return carry

        lax.fori_loop(1, total_n, drain, 0)


def regroup(sample_rows, destination, own_n, rep_n):
    count, feat = sample_rows.shape
    pp = count // (own_n * rep_n)
    target = destination // count
    outgoing = jnp.zeros((own_n, rep_n, pp, feat), sample_rows.dtype)
    outgoing = outgoing.at[target // rep_n, target % rep_n, destination % pp].set(sample_rows)
    arrived = lax.all_to_all(
        lax.all_to_all(outgoing, "own", split_axis=0, concat_axis=0, tiled=True),
        "rep", split_axis=1, concat_axis=1, tiled=True,
    )
    return arrived.reshape(count, feat)


def per_device(sample_rows, destination, neighbours, centroids):
    own_n = lax.axis_size("own")
    rep_n = lax.axis_size("rep")
    count, feat = sample_rows.shape
    blk, _, cb, _ = centroids.shape
    pp = count // (own_n * rep_n)
    chunk = min(256, count)
    nchunk = count // chunk
    fused = pp % 16 == 0 and pp & (pp - 1) == 0 and chunk % pp == 0
    rows = sample_rows if fused else regroup(sample_rows, destination, own_n, rep_n)
    order = [j for j in (2, 1, 3) if j < nchunk] + list(range(4, nchunk)) + [0]
    wc = (blk + 2) * cb
    total_n = own_n * rep_n
    dma = pltpu.SemaphoreType.DMA
    vmem = pl.BlockSpec(memory_space=pltpu.VMEM)
    staged = count if fused else 16
    out, cost = pl.pallas_call(
        functools.partial(kernel, fused, own_n, rep_n, pp, chunk, order),
        out_shape=(
            jax.ShapeDtypeStruct((blk * cb, feat), BF16),
            jax.ShapeDtypeStruct((nchunk, chunk), F32),
        ),
        in_specs=[vmem] * 4,
        out_specs=(vmem, vmem),
        scratch_shapes=[
            pltpu.VMEM((staged, feat), BF16),
            pltpu.VMEM((staged, feat), BF16),
            pltpu.VMEM((wc, feat), BF16),
            pltpu.VMEM((wc, 1), F32),
            pltpu.VMEM((nchunk, 8, chunk), F32),
            pltpu.VMEM((nchunk, 8, chunk), F32),
            pltpu.VMEM((wc, feat), F32),
            pltpu.VMEM((wc, 128), F32),
            pltpu.VMEM((nchunk, wc, chunk), F32),
            pltpu.VMEM((nchunk, wc, chunk), BF16),
            pltpu.VMEM((2, 3, cb, feat), BF16),
            pltpu.VMEM((2, 3, cb, feat), BF16),
            pltpu.VMEM((2, 3, 8, 128), F32),
            pltpu.VMEM((2, 3, 8, 128), F32),
            dma((total_n,)),
            dma((total_n,)),
            dma((2,)),
            dma((2,)),
            dma((2, 3)),
            dma((2, 3)),
            dma((2, 3)),
            dma((2, 3)),
        ],
        compiler_params=pltpu.CompilerParams(
            collective_id=0, has_side_effects=True, vmem_limit_bytes=48 * 1024 * 1024
        ),
    )(neighbours.T, destination.reshape(1, count), rows, centroids.reshape(blk * cb, feat))
    return out.reshape(centroids.shape), cost.reshape(count)


def solution(mesh):
    return jax.shard_map(
        per_device,
        mesh=mesh,
        in_specs=(
            P(("own", "rep"), None),
            P(("own", "rep")),
            P(("own", "rep"), None),
            P("own", "rep", None, None),
        ),
        out_specs=(P("own", "rep", None, None), P(("own", "rep"))),
        check_vma=False,
    )
```

time: 140 us -> 84.8 us (0.61)
  the two profiles are of different devices: /device:TPU:16 before, /device:TPU:17 now
where the time goes in v1:
time: 84.8 us; the launch traced here: 83.6 us
  Pallas kernels  77.6 us (92%)
  local copies, waits for them, and re-layouts  5.41 us (6%)
    pallas_call x1, Pallas kernels, per_device(): pl.pallas_call(functools.partial(kernel, fused, own_n, rep_n, pp, chunk,...  77.6 us
    unnamed x10, local copies, waits for them, and re-layouts  5.41 us

profile of v1, /device:TPU:17, one launch (start us, length us, event | category | flops | bytes accessed | tf_op | source)
XLA Modules:
  0.0 83.6 jit_solution(16241002030008345015)
XLA Ops:
  0.6 0.0 copy-start
  0.6 1.4 %copy-done = bf16[1024,768]{1,0:T(8,128)(2,1)S(1)} copy-done((bf16[1024,768]{1,0:T(8,128)(2,1)S(1)}, bf16[1024,768]{1,0:T(8,128)(2,1)}, u32[]{:S(2)}) %copy-start) | copy-done | bytes 1572888
  2.0 0.0 copy-start.1
  2.0 1.1 %copy-done.1 = bf16[4,1,128,768]{3,2,1,0:T(8,128)(2,1)S(1)} copy-done((bf16[4,1,128,768]{3,2,1,0:T(8,128)(2,1)S(1)}, bf16[4,1,128,768]{3,2,1,0:T(8,128)(2,1)}, u32[]{:S(2)}) %copy-start.1) | copy-done | bytes 786456
  3.2 0.0 copy-start.2
  3.2 0.7 copy-done.2
  3.9 0.0 copy-start.3
  3.9 0.7 copy-done.3
  4.6 77.6 %shard_map.59 = (bf16[512,768]{1,0:T(8,128)(2,1)S(1)}, f32[4,256]{1,0:T(4,128)S(1)}) custom-call(s32[4,1024]{1,0:T(4,128)S(1)} %bitcast.10, s32[1,1024]{1,0:T(1,128)S(1)} %bitcast.11, bf16[1024,768]{1,0:T(8,128)(2,1)S(1)} %copy-done, bf16[512,768]{1,0:T(8,128)(2,1)S(1)} %bitcast.9), custom_call_target="tpu_custom_call" | custom-call | tf_op jit(solution)/shard_map/pallas_call | solution.py:359
  82.1 0.6 copy.7
  82.7 0.9 %copy.9 = bf16[4,1,128,768]{3,2,1,0:T(8,128)(2,1)} copy(bf16[4,1,128,768]{3,2,1,0:T(8,128)(2,1)S(1)} %bitcast.8) | data formatting | bytes 1572864
Async XLA Ops:
  0.6 1.4 %copy-start = (bf16[1024,768]{1,0:T(8,128)(2,1)S(1)}, bf16[1024,768]{1,0:T(8,128)(2,1)}, u32[]{:S(2)}) copy-start(bf16[1024,768]{1,0:T(8,128)(2,1)} %refs_2_.1) | copy-start | bytes 4718596
  2.0 1.1 %copy-start.1 = (bf16[4,1,128,768]{3,2,1,0:T(8,128)(2,1)S(1)}, bf16[4,1,128,768]{3,2,1,0:T(8,128)(2,1)}, u32[]{:S(2)}) copy-start(bf16[4,1,128,768]{3,2,1,0:T(8,128)(2,1)} %param.7) | copy-start | bytes 2359300
  3.2 0.7 copy-start.2
  3.9 0.7 copy-start.3

commit v2 on v1

--- a/solution.py
+++ b/solution.py
@@ -25,13 +25,13 @@
 def kernel(
     fused, own_n, rep_n, pp, chunk, order, *refs
 ):
-    (nbr_ref, dest_ref, rows_ref, cent_ref, out_ref, cost_ref,
-     arr, outb, cand, cn, bias, xn, acc, macc, lg, resp, snd, rcv, msnd, mrcv,
-     a_send, a_recv, c_send, c_recv, s_send, s_recv, m_send, m_recv) = refs
-    count, feat = rows_ref.shape
+    (nbr_in, dest_in, rows_in, cent_in, out_ref, cost_ref,
+     nbr_ref, dest_ref, rows_ref, arr, outb, stat, cand, cn, bias, xn, acc, macc, lg, resp, snd, rcv, msnd, mrcv,
+     a_send, a_recv, c_send, c_recv, s_send, s_recv, m_send, m_recv, load) = refs
+    count, feat = rows_in.shape
     slots = nbr_ref.shape[0]
     cb = rcv.shape[2]
-    blk = cent_ref.shape[0] // cb
+    blk = cent_in.shape[0] // cb
     win = blk + 2
     wc = win * cb
     nchunk = count // chunk
@@ -42,6 +42,17 @@
     sides = (own > 0, own < own_n - 1)
     scale2 = 0.5 / math.sqrt(feat) / LN2
 
+    loads = [
+        pltpu.make_async_copy(a, b, load.at[i])
+        for i, (a, b) in enumerate((
+            (dest_in, dest_ref),
+            (rows_in, rows_ref if fused else arr),
+            (cent_in, cand.at[pl.ds(cb, blk * cb)]),
+            (nbr_in, nbr_ref),
+        ))
+    ]
+    for one in loads:
+        one.start()
     barrier = pltpu.get_barrier_semaphore()
     if fused:
         def greet(k, carry):
@@ -69,13 +80,12 @@
             for q in range(3):
                 rcv[d, q] = zero_block
                 mrcv[d, q] = jnp.zeros((8, 128), F32)
-    cand[cb : (blk + 1) * cb, :] = cent_ref[...]
 
     def block_copy(d):
         src = 0 if d == 0 else (blk - 1) * cb
         dst = (win - 1) * cb if d == 0 else 0
         return pltpu.make_async_remote_copy(
-            src_ref=cent_ref.at[pl.ds(src, cb)],
+            src_ref=cent_in.at[pl.ds(src, cb)],
             dst_ref=cand.at[pl.ds(dst, cb)],
             send_sem=c_send.at[d],
             recv_sem=c_recv.at[d],
@@ -140,6 +150,8 @@
 
         lax.fori_loop(0, per, send, 0)
 
+    loads[0].wait()
+    loads[1].wait()
     if fused:
         for n, j in enumerate(order):
             g = lax.rem(group + j, nchunk)
@@ -149,10 +161,11 @@
             send_group(g)
         mine = pl.ds(pl.multiple_of(me * pp, pp), pp)
         arr[mine, :] = outb[mine, :]
-        rows = arr
     else:
         wait_entry()
-        rows = rows_ref
+    rows = arr
+    loads[2].wait()
+    loads[3].wait()
 
     for c in range(nchunk):
         ids = nbr_ref[:, c * chunk : (c + 1) * chunk]
@@ -177,6 +190,12 @@
             block_copy(d).wait_recv()
     norms(0, cb)
     norms(wc - cb, wc)
+
+    def fold(got):
+        folded = got[:, 0:128]
+        for i in range(1, chunk // 128):
+            folded = folded + got[:, i * 128 : (i + 1) * 128]
+        return folded
 
     def respond(c):
         raw = [lg[c, w * cb : (w + 1) * cb, :] + bias[c, w : w + 1, :] for w in range(win)]
@@ -189,11 +208,7 @@
             part = slice(w * cb, (w + 1) * cb)
             got = raw[w] * inverse
             resp[c, part, :] = got.astype(BF16)
-            folded = got[:, 0:128]
-            for i in range(1, chunk // 128):
-                folded = folded + got[:, i * 128 : (i + 1) * 128]
-            macc[part, :] += folded
-        return top, whole
+            macc[part, :] += fold(got)
 
     def chunk_rows(c):
         return rows[pl.ds(pl.multiple_of(c * chunk, chunk), chunk), :]
@@ -280,15 +295,43 @@
     for w in range(2, win - 2):
         cand[part_of(w), :] = fresh(w)
         score(w)
-    for d, q, w in ((1, 0, 1), (0, 0, win - 2), (1, 1, 0), (0, 1, win - 1)):
+    def update(d, q, w):
         land(d, q)
         cand[part_of(w), :] = fresh(w, (d, q))
         score(w)
 
+    update(1, 0, 1)
+    update(0, 0, win - 2)
+
+    def inner(c, carry):
+        raw = [lg[c, part_of(w), :] + bias[c, w : w + 1, :] for w in range(1, win - 1)]
+        top = jnp.max(functools.reduce(jnp.maximum, raw), axis=0, keepdims=True)
+        raw = [jnp.exp2(r - top) for r in raw]
+        for w in range(1, win - 1):
+            lg[c, part_of(w), :] = raw[w - 1]
+        stat[c, 0:1, :] = top
+        stat[c, 1:2, :] = jnp.sum(functools.reduce(jnp.add, raw), axis=0, keepdims=True)
+        return carry
+
+    lax.fori_loop(0, nchunk, inner, 0)
+    update(1, 1, 0)
+    update(0, 1, win - 1)
     macc[...] = jnp.zeros_like(macc)
 
     def second(c, carry):
-        top, whole = respond(c)
+        ends = (0, win - 1)
+        raw = [lg[c, part_of(w), :] + bias[c, w : w + 1, :] for w in ends]
+        held = stat[c, 0:1, :]
+        top = jnp.maximum(jnp.max(jnp.maximum(*raw), axis=0, keepdims=True), held)
+        raw = [jnp.exp2(r - top) for r in raw]
+        factor = jnp.exp2(held - top)
+        whole = stat[c, 1:2, :] * factor + jnp.sum(raw[0] + raw[1], axis=0, keepdims=True)
+        inverse = 1.0 / whole
+        factor = factor * inverse
+        for w in range(win):
+            got = raw[ends.index(w)] * inverse if w in ends else lg[c, part_of(w), :] * factor
+            resp[c, part_of(w), :] = got.astype(BF16)
+            macc[part_of(w), :] += fold(got)
         cost_ref[pl.ds(c, 1), :] = xn[c][0:1, :] * (scale2 * LN2) - (top * LN2 + jnp.log(whole))
         return carry
 
@@ -362,11 +405,15 @@
             jax.ShapeDtypeStruct((blk * cb, feat), BF16),
             jax.ShapeDtypeStruct((nchunk, chunk), F32),
         ),
-        in_specs=[vmem] * 4,
+        in_specs=[pl.BlockSpec(memory_space=pl.ANY)] * 4,
         out_specs=(vmem, vmem),
         scratch_shapes=[
+            pltpu.VMEM((neighbours.shape[1], count), jnp.int32),
+            pltpu.VMEM((1, count), jnp.int32),
             pltpu.VMEM((staged, feat), BF16),
+            pltpu.VMEM((count, feat), BF16),
             pltpu.VMEM((staged, feat), BF16),
+            pltpu.VMEM((nchunk, 8, chunk), F32),
             pltpu.VMEM((wc, feat), BF16),
             pltpu.VMEM((wc, 1), F32),
             pltpu.VMEM((nchunk, 8, chunk), F32),
@@ -387,6 +434,7 @@
             dma((2, 3)),
             dma((2, 3)),
             dma((2, 3)),
+            dma((4,)),
         ],
         compiler_params=pltpu.CompilerParams(
             collective_id=0, has_side_effects=True, vmem_limit_bytes=48 * 1024 * 1024

time: 84.8 us -> 84.7 us (level)
  no operation moved by 1% of the time
where the time goes in v2:
time: 84.7 us; the launch traced here: 83.5 us
  Pallas kernels  77.4 us (91%)
  local copies, waits for them, and re-layouts  5.41 us (6%)
    pallas_call x1, Pallas kernels, per_device(): pl.pallas_call(functools.partial(kernel, fused, own_n, rep_n, pp, chunk,...  77.4 us
    unnamed x10, local copies, waits for them, and re-layouts  5.41 us

profile of v2, /device:TPU:17, one launch (start us, length us, event | category | flops | bytes accessed | tf_op | source)
XLA Modules:
  0.0 83.5 jit_solution(10636665792997372330)
XLA Ops:
  0.6 0.0 copy-start
  0.6 1.4 %copy-done = bf16[1024,768]{1,0:T(8,128)(2,1)S(1)} copy-done((bf16[1024,768]{1,0:T(8,128)(2,1)S(1)}, bf16[1024,768]{1,0:T(8,128)(2,1)}, u32[]{:S(2)}) %copy-start) | copy-done | bytes 1572888
  2.0 0.0 copy-start.1
  2.0 1.1 %copy-done.1 = bf16[4,1,128,768]{3,2,1,0:T(8,128)(2,1)S(1)} copy-done((bf16[4,1,128,768]{3,2,1,0:T(8,128)(2,1)S(1)}, bf16[4,1,128,768]{3,2,1,0:T(8,128)(2,1)}, u32[]{:S(2)}) %copy-start.1) | copy-done | bytes 786456
  3.2 0.0 copy-start.2
  3.2 0.7 copy-done.2
  3.9 0.0 copy-start.3
  3.9 0.7 copy-done.3
  4.6 77.4 %shard_map.59 = (bf16[512,768]{1,0:T(8,128)(2,1)S(1)}, f32[4,256]{1,0:T(4,128)S(1)}) custom-call(s32[4,1024]{1,0:T(4,128)S(1)} %bitcast.10, s32[1,1024]{1,0:T(1,128)S(1)} %bitcast.11, bf16[1024,768]{1,0:T(8,128)(2,1)S(1)} %copy-done, bf16[512,768]{1,0:T(8,128)(2,1)S(1)} %bitcast.9), custom_call_target="tpu_custom_call" | custom-call | tf_op jit(solution)/shard_map/pallas_call | solution.py:402
  82.0 0.6 copy.7
  82.6 0.9 %copy.9 = bf16[4,1,128,768]{3,2,1,0:T(8,128)(2,1)} copy(bf16[4,1,128,768]{3,2,1,0:T(8,128)(2,1)S(1)} %bitcast.8) | data formatting | bytes 1572864
Async XLA Ops:
  0.6 1.4 %copy-start = (bf16[1024,768]{1,0:T(8,128)(2,1)S(1)}, bf16[1024,768]{1,0:T(8,128)(2,1)}, u32[]{:S(2)}) copy-start(bf16[1024,768]{1,0:T(8,128)(2,1)} %refs_2_.1) | copy-start | bytes 4718596
  2.0 1.1 %copy-start.1 = (bf16[4,1,128,768]{3,2,1,0:T(8,128)(2,1)S(1)}, bf16[4,1,128,768]{3,2,1,0:T(8,128)(2,1)}, u32[]{:S(2)}) copy-start(bf16[4,1,128,768]{3,2,1,0:T(8,128)(2,1)} %param.7) | copy-start | bytes 2359300
  3.2 0.7 copy-start.2
  3.9 0.7 copy-start.3

commit v3 on v2

--- a/solution.py
+++ b/solution.py
@@ -27,7 +27,8 @@
 ):
     (nbr_in, dest_in, rows_in, cent_in, out_ref, cost_ref,
      nbr_ref, dest_ref, rows_ref, arr, outb, stat, cand, cn, bias, xn, acc, macc, lg, resp, snd, rcv, msnd, mrcv,
-     a_send, a_recv, c_send, c_recv, s_send, s_recv, m_send, m_recv, load) = refs
+     a_send, a_recv, c_send, c_recv, s_send, s_recv, m_send, m_recv, load,
+     t_send, t_recv, f_send, f_recv, res, res_cost) = refs
     count, feat = rows_in.shape
     slots = nbr_ref.shape[0]
     cb = rcv.shape[2]
@@ -35,11 +36,25 @@
     win = blk + 2
     wc = win * cb
     nchunk = count // chunk
+    lanes = chunk // 128
     total_n = own_n * rep_n
     own = lax.axis_index("own")
     rep = lax.axis_index("rep")
     me = own * rep_n + rep
-    sides = (own > 0, own < own_n - 1)
+    paired = fused and rep_n == 2 and own_n % 2 == 0
+
+    def place_of(a, b):
+        if not paired:
+            return (a, b)
+        odd = lax.rem(a, 2)
+        return (a - odd + b, odd)
+
+    work, col = place_of(own, rep)
+    wid = work * rep_n + col
+    moved = jnp.logical_and(paired, wid != me)
+    stays = jnp.logical_not(moved)
+    holds = (own > 0, own < own_n - 1)
+    sides = (work > 0, work < own_n - 1)
     scale2 = 0.5 / math.sqrt(feat) / LN2
 
     loads = [
@@ -51,8 +66,31 @@
             (nbr_in, nbr_ref),
         ))
     ]
-    for one in loads:
+    def on(which, fn):
+        if paired or which is stays:
+            pl.when(which)(fn)
+
+    def traded(src, dst, i, send=t_send, recv=t_recv):
+        return pltpu.make_async_remote_copy(
+            src_ref=src, dst_ref=dst, send_sem=send.at[i], recv_sem=recv.at[i],
+            device_id=(work, col), device_id_type=MESH,
+        )
+
+    def trades():
+        return [
+            traded(nbr_in, nbr_ref, 0),
+            traded(cent_in, cand.at[pl.ds(cb, blk * cb)], 1),
+        ]
+
+    def each(ops, act):
+        def run():
+            for one in ops():
+                act(one)
+        return run
+
+    for one in loads[:2]:
         one.start()
+    on(stays, each(lambda: loads[2:], lambda one: one.start()))
     barrier = pltpu.get_barrier_semaphore()
     if fused:
         def greet(k, carry):
@@ -89,12 +127,12 @@
             dst_ref=cand.at[pl.ds(dst, cb)],
             send_sem=c_send.at[d],
             recv_sem=c_recv.at[d],
-            device_id=(own + 2 * d - 1, rep),
+            device_id=place_of(own + 2 * d - 1, rep),
             device_id_type=MESH,
         )
 
     def edge_copies(d, q):
-        where = (own + 2 * d - 1, rep)
+        where = place_of(work + 2 * d - 1, col)
         return [
             pltpu.make_async_remote_copy(
                 src_ref=a.at[d, q], dst_ref=b.at[d, q], send_sem=s.at[d, q], recv_sem=r.at[d, q],
@@ -109,7 +147,7 @@
             dst_ref=arr.at[pl.ds(pl.multiple_of(src * pp, pp), pp)],
             send_sem=a_send.at[t],
             recv_sem=a_recv.at[src],
-            device_id=(lax.div(t, rep_n), lax.rem(t, rep_n)),
+            device_id=place_of(lax.div(t, rep_n), lax.rem(t, rep_n)),
             device_id_type=MESH,
         )
 
@@ -133,8 +171,9 @@
                 @pl.when(sides[d])
                 def _():
                     pl.semaphore_wait(barrier, 1)
+        on(moved, each(trades, lambda one: one.start()))
         for d in range(2):
-            @pl.when(sides[d])
+            @pl.when(holds[d])
             def _():
                 block_copy(d).start()
 
@@ -142,7 +181,7 @@
         def send(k, carry):
             t = g * per + lax.rem(me + k, per)
 
-            @pl.when(t != me)
+            @pl.when(t != wid)
             def _():
                 row_copy(me, t).start()
 
@@ -160,17 +199,18 @@
                 wait_entry()
             send_group(g)
         mine = pl.ds(pl.multiple_of(me * pp, pp), pp)
-        arr[mine, :] = outb[mine, :]
+        kept = pl.ds(pl.multiple_of(wid * pp, pp), pp)
+        arr[mine, :] = outb[kept, :]
     else:
         wait_entry()
     rows = arr
-    loads[2].wait()
-    loads[3].wait()
+    on(stays, each(lambda: loads[2:], lambda one: one.wait()))
+    on(moved, each(trades, lambda one: one.wait_recv()))
 
     for c in range(nchunk):
         ids = nbr_ref[:, c * chunk : (c + 1) * chunk]
         for w in range(win):
-            block = (own * blk - 1 + w) * rep_n + rep
+            block = (work * blk - 1 + w) * rep_n + col
             hit = ids[0:1] == block
             for m in range(1, slots):
                 hit = jnp.logical_or(hit, ids[m : m + 1] == block)
@@ -332,7 +372,9 @@
             got = raw[ends.index(w)] * inverse if w in ends else lg[c, part_of(w), :] * factor
             resp[c, part_of(w), :] = got.astype(BF16)
             macc[part_of(w), :] += fold(got)
-        cost_ref[pl.ds(c, 1), :] = xn[c][0:1, :] * (scale2 * LN2) - (top * LN2 + jnp.log(whole))
+        cost = xn[c][0:1, :] * (scale2 * LN2) - (top * LN2 + jnp.log(whole))
+        for i in range(lanes):
+            res_cost[pl.ds(c * lanes + i, 1), :] = cost[:, i * 128 : (i + 1) * 128]
         return carry
 
     lax.fori_loop(0, nchunk, second, 0)
@@ -343,28 +385,59 @@
             sums = sums + dot(resp[c, part_of(w), :], chunk_rows(c), NN)
         acc[part_of(w), :] = sums
 
+    on(moved, each(lambda: [traded(res_cost, cost_ref, 3, f_send, f_recv)], lambda one: one.start()))
     for d, w in ((0, 0), (1, win - 1)):
         gather(w)
         ship(d, 2, w)
     for w in range(1, win - 1):
         gather(w)
+    def give(n):
+        low, high = ((cb, (blk - 1) * cb), (0, cb), ((blk - 1) * cb, blk * cb))[n]
+        part = pl.ds(low, high - low)
+
+        def here():
+            out_ref[part, :] = res[part, :]
+
+        on(stays, here)
+        on(moved, each(lambda: [given(n)], lambda one: one.start()))
+
+    def given(n):
+        if n == 3:
+            return traded(res_cost, cost_ref, 3, f_send, f_recv)
+        low, high = ((cb, (blk - 1) * cb), (0, cb), ((blk - 1) * cb, blk * cb))[n]
+        part = pl.ds(low, high - low)
+        return traded(res.at[part], out_ref.at[part], n, f_send, f_recv)
+
     for w in range(2, win - 2):
-        out_ref[part_of(w - 1), :] = fresh(w)
-    for d, w in ((1, 1), (0, win - 2)):
+        res[part_of(w - 1), :] = fresh(w)
+    give(0)
+    for n, d, w in ((1, 1, 1), (2, 0, win - 2)):
         land(d, 2)
-        out_ref[part_of(w - 1), :] = fresh(w, (d, 2))
+        res[part_of(w - 1), :] = fresh(w, (d, 2))
+        give(n)
+
+    def cost_here():
+        cost_ref[...] = res_cost[...]
+
+    on(stays, cost_here)
 
     for d in range(2):
+        @pl.when(holds[d])
+        def _():
+            block_copy(d).wait_send()
+
         @pl.when(sides[d])
         def _():
-            block_copy(d).wait_send()
             for q in range(3):
                 for copy in edge_copies(d, q):
                     copy.wait_send()
 
+    on(moved, each(trades, lambda one: one.wait_send()))
+    on(moved, each(lambda: [given(n) for n in range(4)], lambda one: one.wait()))
+
     if fused:
         def drain(k, carry):
-            row_copy(me, lax.rem(me + k, total_n)).wait_send()
+            row_copy(me, lax.rem(wid + k, total_n)).wait_send()
             return carry
 
         lax.fori_loop(1, total_n, drain, 0)
@@ -403,9 +476,9 @@
         functools.partial(kernel, fused, own_n, rep_n, pp, chunk, order),
         out_shape=(
             jax.ShapeDtypeStruct((blk * cb, feat), BF16),
-            jax.ShapeDtypeStruct((nchunk, chunk), F32),
+            jax.ShapeDtypeStruct((count // 128, 128), F32),
         ),
-        in_specs=[pl.BlockSpec(memory_space=pl.ANY)] * 4,
+        in_specs=[pl.BlockSpec(memory_space=pltpu.HBM)] * 4,
         out_specs=(vmem, vmem),
         scratch_shapes=[
             pltpu.VMEM((neighbours.shape[1], count), jnp.int32),
@@ -435,9 +508,15 @@
             dma((2, 3)),
             dma((2, 3)),
             dma((4,)),
+            dma((2,)),
+            dma((2,)),
+            dma((4,)),
+            dma((4,)),
+            pltpu.VMEM((blk * cb, feat), BF16),
+            pltpu.VMEM((count // 128, 128), F32),
         ],
         compiler_params=pltpu.CompilerParams(
-            collective_id=0, has_side_effects=True, vmem_limit_bytes=48 * 1024 * 1024
+            collective_id=0, has_side_effects=True, vmem_limit_bytes=64 * 1024 * 1024
         ),
     )(neighbours.T, destination.reshape(1, count), rows, centroids.reshape(blk * cb, feat))
     return out.reshape(centroids.shape), cost.reshape(count)

time: 84.7 us -> 76.8 us (0.907); the launches traced: 83.5 us -> 76.6 us
  Pallas kernels: 77.4 us -> 73.3 us
  local copies, waits for them, and re-layouts: 5.41 us -> 2.66 us
    pallas_call x1, Pallas kernels: 77.4 us -> 73.3 us  [per_device(): pl.pallas_call(functools.partial(kernel, fused, own_n, rep_n, pp, chunk,...]
    unnamed x10 -> x4, local copies, waits for them, and re-layouts: 5.41 us -> 2.66 us
where the time goes in v3:
time: 76.8 us; the launch traced here: 76.6 us
  Pallas kernels  73.3 us (95%)
  local copies, waits for them, and re-layouts  2.66 us (3%)
    pallas_call x1, Pallas kernels, per_device(): pl.pallas_call(functools.partial(kernel, fused, own_n, rep_n, pp, chunk,...  73.3 us
    unnamed x4, local copies, waits for them, and re-layouts  2.66 us

profile of v3, /device:TPU:17, one launch (start us, length us, event | category | flops | bytes accessed | tf_op | source)
XLA Modules:
  0.0 76.6 jit_solution(2901020680957354075)
XLA Ops:
  0.6 73.3 %shard_map.59 = (bf16[512,768]{1,0:T(8,128)(2,1)}, f32[8,128]{1,0:T(8,128)}) custom-call(s32[4,1024]{1,0:T(4,128)} %bitcast.9, s32[1,1024]{1,0:T(1,128)} %bitcast.10, bf16[1024,768]{1,0:T(8,128)(2,1)} %refs_2_.1, bf16[512,768]{1,0:T(8,128)(2,1)} %bitcast.8), custom_call_target="tpu_custom_call" | custom-call | tf_op jit(solution)/shard_map/pallas_call | solution.py:475
  74.0 0.0 copy-start
  74.0 2.1 %copy.9 = bf16[4,1,128,768]{3,2,1,0:T(8,128)(2,1)} copy(bf16[4,1,128,768]{3,2,1,0:T(8,128)(2,1)} %bitcast.7) | data formatting | bytes 1572864
  76.0 0.0 copy-done
  76.0 0.6 copy.10
Async XLA Ops:
  74.0 2.1 %copy-start = (f32[8,128]{1,0:T(8,128)S(1)}, f32[8,128]{1,0:T(8,128)}, u32[]{:S(2)}) copy-start(f32[8,128]{1,0:T(8,128)} %get-tuple-element.5) | copy-start | bytes 12292

commit v4 on v3

--- a/solution.py
+++ b/solution.py
@@ -219,17 +219,22 @@
     acc[...] = jnp.zeros_like(acc)
     macc[...] = jnp.zeros_like(macc)
 
-    def norms(low, high):
-        wide = cand[low:high, :].astype(F32)
-        cn[low:high, :] = jnp.sum(wide * wide, axis=1, keepdims=True) * scale2
-
-    norms(cb, (blk + 1) * cb)
+    def part_of(w):
+        if isinstance(w, int):
+            return pl.ds(w * cb, cb)
+        return pl.ds(pl.multiple_of(w * cb, cb), cb)
+
+    def norms(part):
+        wide = cand[part, :].astype(F32)
+        cn[part, :] = jnp.sum(wide * wide, axis=1, keepdims=True) * scale2
+
+    norms(pl.ds(cb, blk * cb))
     for d in range(2):
         @pl.when(sides[1 - d])
         def _():
             block_copy(d).wait_recv()
-    norms(0, cb)
-    norms(wc - cb, wc)
+    norms(part_of(0))
+    norms(part_of(win - 1))
 
     def fold(got):
         folded = got[:, 0:128]
@@ -286,9 +291,6 @@
     last = lax.rem(group + nchunk - 1, nchunk)
     arrive(last)
 
-    def part_of(w):
-        return slice(w * cb, (w + 1) * cb)
-
     def mass_of(w):
         return jnp.sum(macc[part_of(w), :], axis=1, keepdims=True)
 
@@ -297,13 +299,17 @@
         wide = jnp.transpose(jnp.broadcast_to(mass_of(w), (cb, 128)))
         msnd[d, q] = wide[0:8, :]
 
-        @pl.when(sides[d])
+        there = work + 2 * d - 1
+
+        @pl.when(jnp.logical_and(there >= 0, there < own_n))
         def _():
             for copy in edge_copies(d, q):
                 copy.start()
 
     def land(d, q):
-        @pl.when(sides[1 - d])
+        there = work + 1 - 2 * d
+
+        @pl.when(jnp.logical_and(there >= 0, there < own_n))
         def _():
             for copy in edge_copies(d, q):
                 copy.wait_recv()
@@ -321,13 +327,17 @@
         acc[part_of(w), :] += dot(resp[last, part_of(w), :], chunk_rows(last), NN)
 
     def score(w):
-        norms(w * cb, (w + 1) * cb)
+        norms(part_of(w))
         for c in range(nchunk):
             lg[c, part_of(w), :] = (
                 dot(cand[part_of(w), :], chunk_rows(c), NT) * (2.0 * scale2) - cn[part_of(w), :]
             )
 
-    for d, q, w in ((0, 0, 0), (1, 0, win - 1), (0, 1, 1), (1, 1, win - 2)):
+    odd = lax.rem(work, 2)
+    even = 1 - odd
+    far_out, far_in = odd * (win - 1), 1 + odd * (win - 3)
+    near_out, near_in = even * (win - 1), 1 + even * (win - 3)
+    for d, q, w in ((odd, 0, far_out), (odd, 1, far_in), (even, 0, near_out), (even, 1, near_in)):
         finish(w)
         ship(d, q, w)
     for w in range(2, win - 2):
@@ -340,8 +350,9 @@
         cand[part_of(w), :] = fresh(w, (d, q))
         score(w)
 
-    update(1, 0, 1)
-    update(0, 0, win - 2)
+    update(odd, 0, near_in)
+    update(odd, 1, near_out)
+    update(even, 0, far_in)
 
     def inner(c, carry):
         raw = [lg[c, part_of(w), :] + bias[c, w : w + 1, :] for w in range(1, win - 1)]
@@ -354,8 +365,7 @@
         return carry
 
     lax.fori_loop(0, nchunk, inner, 0)
-    update(1, 1, 0)
-    update(0, 1, win - 1)
+    update(even, 1, far_out)
     macc[...] = jnp.zeros_like(macc)
 
     def second(c, carry):
@@ -385,36 +395,35 @@
             sums = sums + dot(resp[c, part_of(w), :], chunk_rows(c), NN)
         acc[part_of(w), :] = sums
 
-    on(moved, each(lambda: [traded(res_cost, cost_ref, 3, f_send, f_recv)], lambda one: one.start()))
-    for d, w in ((0, 0), (1, win - 1)):
-        gather(w)
-        ship(d, 2, w)
-    for w in range(1, win - 1):
-        gather(w)
-    def give(n):
-        low, high = ((cb, (blk - 1) * cb), (0, cb), ((blk - 1) * cb, blk * cb))[n]
-        part = pl.ds(low, high - low)
+    on(moved, each(lambda: [traded(res_cost, cost_ref, blk, f_send, f_recv)], lambda one: one.start()))
+    def given(n, w):
+        part = part_of(w - 1)
+        return traded(res.at[part], out_ref.at[part], n, f_send, f_recv)
+
+    def give(n, w):
+        part = part_of(w - 1)
 
         def here():
             out_ref[part, :] = res[part, :]
 
         on(stays, here)
-        on(moved, each(lambda: [given(n)], lambda one: one.start()))
-
-    def given(n):
-        if n == 3:
-            return traded(res_cost, cost_ref, 3, f_send, f_recv)
-        low, high = ((cb, (blk - 1) * cb), (0, cb), ((blk - 1) * cb, blk * cb))[n]
-        part = pl.ds(low, high - low)
-        return traded(res.at[part], out_ref.at[part], n, f_send, f_recv)
-
+        on(moved, each(lambda: [given(n, w)], lambda one: one.start()))
+
+    gather(far_out)
+    ship(odd, 2, far_out)
     for w in range(2, win - 2):
+        gather(w)
         res[part_of(w - 1), :] = fresh(w)
-    give(0)
-    for n, d, w in ((1, 1, 1), (2, 0, win - 2)):
+        give(w, w)
+        if w == 2:
+            gather(near_out)
+            ship(even, 2, near_out)
+    gather(near_in)
+    gather(far_in)
+    for n, d, w in ((0, odd, near_in), (1, even, far_in)):
         land(d, 2)
         res[part_of(w - 1), :] = fresh(w, (d, 2))
-        give(n)
+        give(n, w)
 
     def cost_here():
         cost_ref[...] = res_cost[...]
@@ -433,7 +442,12 @@
                     copy.wait_send()
 
     on(moved, each(trades, lambda one: one.wait_send()))
-    on(moved, each(lambda: [given(n) for n in range(4)], lambda one: one.wait()))
+    def returned():
+        for n in range(blk + 1):
+            one = given(n, 1) if n < blk else traded(res_cost, cost_ref, blk, f_send, f_recv)
+            one.wait()
+
+    on(moved, returned)
 
     if fused:
         def drain(k, carry):
@@ -510,8 +524,8 @@
             dma((4,)),
             dma((2,)),
             dma((2,)),
-            dma((4,)),
-            dma((4,)),
+            dma((blk + 1,)),
+            dma((blk + 1,)),
             pltpu.VMEM((blk * cb, feat), BF16),
             pltpu.VMEM((count // 128, 128), F32),
         ],

time: 76.8 us -> 74.9 us (0.975)
  Pallas kernels: 73.3 us -> 71.4 us
    pallas_call x1, Pallas kernels: 73.3 us -> 71.4 us  [per_device(): pl.pallas_call(functools.partial(kernel, fused, own_n, rep_n, pp, chunk,...]
where the time goes in v4:
time: 74.9 us; the launch traced here: 74.7 us
  Pallas kernels  71.4 us (95%)
  local copies, waits for them, and re-layouts  2.66 us (4%)
    pallas_call x1, Pallas kernels, per_device(): pl.pallas_call(functools.partial(kernel, fused, own_n, rep_n, pp, chunk,...  71.4 us
    unnamed x4, local copies, waits for them, and re-layouts  2.66 us

profile of v4, /device:TPU:17, one launch (start us, length us, event | category | flops | bytes accessed | tf_op | source)
XLA Modules:
  0.0 74.7 jit_solution(16588567916245577548)
XLA Ops:
  0.6 71.4 %shard_map.59 = (bf16[512,768]{1,0:T(8,128)(2,1)}, f32[8,128]{1,0:T(8,128)}) custom-call(s32[4,1024]{1,0:T(4,128)} %bitcast.9, s32[1,1024]{1,0:T(1,128)} %bitcast.10, bf16[1024,768]{1,0:T(8,128)(2,1)} %refs_2_.1, bf16[512,768]{1,0:T(8,128)(2,1)} %bitcast.8), custom_call_target="tpu_custom_call" | custom-call | tf_op jit(solution)/shard_map/pallas_call | solution.py:489
  72.1 0.0 copy-start
  72.1 2.1 %copy.9 = bf16[4,1,128,768]{3,2,1,0:T(8,128)(2,1)} copy(bf16[4,1,128,768]{3,2,1,0:T(8,128)(2,1)} %bitcast.7) | data formatting | bytes 1572864
  74.1 0.0 copy-done
  74.1 0.6 copy.10
Async XLA Ops:
  72.1 2.1 %copy-start = (f32[8,128]{1,0:T(8,128)S(1)}, f32[8,128]{1,0:T(8,128)}, u32[]{:S(2)}) copy-start(f32[8,128]{1,0:T(8,128)} %get-tuple-element.5) | copy-start | bytes 12292

commit v5 on v4

--- a/solution.py
+++ b/solution.py
@@ -280,15 +280,20 @@
         ones = jnp.ones((8, feat), BF16)
         xn[c] = dot(ones, high, NT) + dot(ones, low, NT)
 
+    def taken(j):
+        if nchunk != 4:
+            return j
+        return jnp.where(j == 3, 1, jnp.where(j == 0, 0, j + 1))
+
     def early(j, carry):
-        c = lax.rem(group + j, nchunk)
+        c = lax.rem(group + taken(j), nchunk)
         arrive(c)
         acc[...] += dot(resp[c], chunk_rows(c), NN)
         return carry
 
     if nchunk > 1:
         lax.fori_loop(0, nchunk - 1, early, 0)
-    last = lax.rem(group + nchunk - 1, nchunk)
+    last = lax.rem(group + taken(nchunk - 1), nchunk)
     arrive(last)
 
     def mass_of(w):
@@ -480,7 +485,7 @@
     nchunk = count // chunk
     fused = pp % 16 == 0 and pp & (pp - 1) == 0 and chunk % pp == 0
     rows = sample_rows if fused else regroup(sample_rows, destination, own_n, rep_n)
-    order = [j for j in (2, 1, 3) if j < nchunk] + list(range(4, nchunk)) + [0]
+    order = [2, 0, 1, 3] if nchunk == 4 else list(range(nchunk))
     wc = (blk + 2) * cb
     total_n = own_n * rep_n
     dma = pltpu.SemaphoreType.DMA

time: 74.9 us -> 75.6 us (level)
  no operation moved by 1% of the time
where the time goes in v5:
time: 75.6 us; the launch traced here: 75.3 us
  Pallas kernels  72 us (95%)
  local copies, waits for them, and re-layouts  2.66 us (4%)
    pallas_call x1, Pallas kernels, per_device(): pl.pallas_call(functools.partial(kernel, fused, own_n, rep_n, pp, chunk,...  72 us
    unnamed x4, local copies, waits for them, and re-layouts  2.66 us

profile of v5, /device:TPU:17, one launch (start us, length us, event | category | flops | bytes accessed | tf_op | source)
XLA Modules:
  0.0 75.3 jit_solution(3921634965537748916)
XLA Ops:
  0.6 72.0 %shard_map.59 = (bf16[512,768]{1,0:T(8,128)(2,1)}, f32[8,128]{1,0:T(8,128)}) custom-call(s32[4,1024]{1,0:T(4,128)} %bitcast.9, s32[1,1024]{1,0:T(1,128)} %bitcast.10, bf16[1024,768]{1,0:T(8,128)(2,1)} %refs_2_.1, bf16[512,768]{1,0:T(8,128)(2,1)} %bitcast.8), custom_call_target="tpu_custom_call" | custom-call | tf_op jit(solution)/shard_map/pallas_call | solution.py:494
  72.6 0.0 copy-start
  72.7 2.1 %copy.9 = bf16[4,1,128,768]{3,2,1,0:T(8,128)(2,1)} copy(bf16[4,1,128,768]{3,2,1,0:T(8,128)(2,1)} %bitcast.7) | data formatting | bytes 1572864
  74.7 0.0 copy-done
  74.7 0.6 copy.10
Async XLA Ops:
  72.6 2.1 %copy-start = (f32[8,128]{1,0:T(8,128)S(1)}, f32[8,128]{1,0:T(8,128)}, u32[]{:S(2)}) copy-start(f32[8,128]{1,0:T(8,128)} %get-tuple-element.5) | copy-start | bytes 12292
